TPU v7x, 32 devices: a whole 2x2x4 slice. The times are simulated.
32 devices in a mesh: rows: 8 (over y, x, core), cols: 4 (over z).
Axes of the slice: x: 2, y: 2, z: 4, core: 2. Of those that a mesh axis runs over, the one named last changes fastest.
Arguments:
- inputs: bfloat16 [8192, 2048], P(('rows', 'cols')), may hold values from -6 to 6
- lengths: int32 [8], P('rows'), may hold values from 256 to 1024, as said below
- gain_one: float32 [2048], replicated, may hold values from 0.1 to 1.9
- shift_one: float32 [2048], replicated, may hold values from -3 to 3
- projection: bfloat16 [2048, 3, 2048], P('rows', None, 'cols'), may hold values from -0.125 to 0.125
- query_bias: float32 [2048], P('cols'), may hold values from -3 to 3
- value_bias: float32 [2048], P('cols'), may hold values from -3 to 3
- out_weight: bfloat16 [2048, 2048], P('cols', 'rows'), may hold values from -0.5 to 0.5
- out_bias: float32 [2048], replicated, may hold values from -3 to 3
- gain_two: float32 [2048], replicated, may hold values from 0.1 to 1.9
- shift_two: float32 [2048], replicated, may hold values from -3 to 3
- up_weight: bfloat16 [2048, 8192], P('rows', 'cols'), may hold values from -0.125 to 0.125
- up_bias: float32 [8192], P('cols'), may hold values from -3 to 3
- down_weight: bfloat16 [8192, 2048], P('cols', 'rows'), may hold values from -0.0625 to 0.0625
- down_bias: float32 [2048], replicated, may hold values from -3 to 3
- cotangent: bfloat16 [8192, 2048], P(('rows', 'cols')), may hold values from -6 to 6
Outputs:
- output: bfloat16 [8192, 2048], P(('rows', 'cols'))
- inputs_grad: float32 [8192, 2048], P(('rows', 'cols'))
- gain_one_grad: float32 [2048], replicated
- shift_one_grad: float32 [2048], replicated
- projection_grad: float32 [2048, 3, 2048], P('rows', None, 'cols')
- query_bias_grad: float32 [2048], P('cols')
- value_bias_grad: float32 [2048], P('cols')
- out_weight_grad: float32 [2048, 2048], P('cols', 'rows')
- out_bias_grad: float32 [2048], replicated
- gain_two_grad: float32 [2048], replicated
- shift_two_grad: float32 [2048], replicated
- up_weight_grad: float32 [2048, 8192], P('rows', 'cols')
- up_bias_grad: float32 [8192], P('cols')
- down_weight_grad: float32 [8192, 2048], P('cols', 'rows')
- down_bias_grad: float32 [2048], replicated
Inputs may be any that keep to these rules, and one draw needn't show every extreme that they name: `lengths`: one sequence has all 1024 slots live and another a quarter of them.
All inputs are finite; a program needn't handle non-finite values.
Results may differ from a plain program's by a relative error of at most 0.02.
Values may be sent and summed in bfloat16 or wider, within the bound.
A program may use at most 256 MiB of HBM per device.

v0:
```python
import math

import jax
import jax.numpy as jnp
from jax import lax
from jax.sharding import PartitionSpec as P

HEADS = 32
HEAD_DIM = 64


epsilon = 1e-05


def normalize(values):
    center = jnp.mean(values, axis=-1, keepdims=True)
    centred = values - center
    spread = jnp.mean(centred * centred, axis=-1, keepdims=True)
    inverse = lax.rsqrt(spread + epsilon)
    return (centred * inverse, inverse)


def norm_back(grad_rows, normed, inverse, gain_row):
    scaled = grad_rows * gain_row
    first_mean = jnp.mean(scaled, axis=-1, keepdims=True)
    second = jnp.mean(scaled * normed, axis=-1, keepdims=True)
    return inverse * (scaled - first_mean - normed * second)


def against(left_rows, right_rows):
    return lax.dot_general(
        left_rows, right_rows, (((1,), (1,)), ((), ())), preferred_element_type=jnp.float32
    )


def outer_sum(left_rows, right_rows):
    return lax.dot_general(
        left_rows, right_rows, (((0,), (0,)), ((), ())), preferred_element_type=jnp.float32
    )


def gelu_slope(before):
    cumulative = 0.5 * (1.0 + lax.erf(before * (1.0 / math.sqrt(2.0))))
    density = jnp.exp(-0.5 * before * before) * (1.0 / math.sqrt(2.0 * math.pi))
    return cumulative + before * density


def score_block(query_rows, key_rows, slopes, seq_length):
    seq_len = query_rows.shape[0]
    positions = jnp.arange(seq_len)
    offset = (positions[None, :] - positions[:, None]).astype(jnp.float32)
    raw_scores = jnp.einsum(
        "qhd,khd->hqk", query_rows, key_rows, preferred_element_type=jnp.float32
    ) * query_rows.shape[2] ** (-0.5)
    scores = raw_scores + slopes[:, None, None] * offset[None, :, :]
    allowed = (positions[None, :] <= positions[:, None]) & (positions[None, :] < seq_length)
    return jnp.where(allowed[None], scores, -1000000000.0)


def fetch_inner(projection, up_weight):
    return (
        lax.all_gather(projection, "rows", axis=0, tiled=True),
        lax.all_gather(up_weight, "rows", axis=0, tiled=True),
    )


def fetch_outer(out_weight, down_weight):
    return (
        lax.all_gather(out_weight, "rows", axis=1, tiled=True),
        lax.all_gather(down_weight, "rows", axis=1, tiled=True),
    )


def gather_normed(rows_local):
    return lax.all_gather(rows_local, "cols", axis=0, tiled=True)


def gather_grads(rows_local):
    return lax.all_gather(rows_local, "cols", axis=0, tiled=True)


def branch_sum(source, weight):
    return lax.psum_scatter(
        jnp.dot(source, weight, preferred_element_type=jnp.float32).astype(jnp.bfloat16),
        "cols",
        scatter_dimension=0,
        tiled=True,
    ).astype(jnp.float32)


def input_sum(source, weight):
    return lax.psum_scatter(
        against(source, weight).astype(jnp.bfloat16), "cols", scatter_dimension=0, tiled=True
    ).astype(jnp.float32)


def per_device(
    inputs,
    lengths,
    gain_one,
    shift_one,
    projection,
    query_bias,
    value_bias,
    out_weight,
    out_bias,
    gain_two,
    shift_two,
    up_weight,
    up_bias,
    down_weight,
    down_bias,
    cotangent,
):
    tok_dev = inputs.shape[0]
    col_count = lax.axis_size("cols")
    col_index = lax.axis_index("cols")
    group_rows = tok_dev * col_count
    seq_count = lengths.shape[0]
    seq_len = group_rows // seq_count
    local_pos = col_index * tok_dev + jnp.arange(tok_dev)
    owning_seq = local_pos // seq_len
    matches = owning_seq[:, None] == jnp.arange(seq_count)[None, :]
    own_length = jnp.sum(jnp.where(matches, lengths[None, :], 0), axis=1)
    live_rows = (local_pos % seq_len < own_length).astype(jnp.float32)[:, None]
    slab_width = projection.shape[2]
    heads_here = slab_width // HEAD_DIM
    head_ids = col_index * heads_here + jnp.arange(heads_here)
    slopes = jnp.exp2(-8.0 * (head_ids + 1).astype(jnp.float32) / HEADS)

    def by_sequence(rows):
        return rows.reshape(seq_count, seq_len, heads_here, HEAD_DIM)

    def forward_one(members):
        query_rows, key_rows, values, seq_length = members
        scores = score_block(query_rows, key_rows, slopes, seq_length)
        highest = jnp.max(scores, axis=-1, keepdims=True)
        raised = jnp.exp(scores - highest)
        summed = jnp.sum(raised, axis=-1, keepdims=True)
        weights = (raised / summed).astype(jnp.bfloat16)
        attended = jnp.einsum("hqk,khd->qhd", weights, values, preferred_element_type=jnp.float32)
        return (attended.astype(jnp.bfloat16), highest + jnp.log(summed))

    def backward_one(members):
        query_rows, key_rows, values, seq_length, log_total, grad_att = members
        scores = score_block(query_rows, key_rows, slopes, seq_length)
        weights = jnp.exp(scores - log_total)
        low_weights = weights.astype(jnp.bfloat16)
        grad_values = jnp.einsum(
            "hqk,qhd->khd", low_weights, grad_att, preferred_element_type=jnp.float32
        )
        grad_weights = jnp.einsum(
            "qhd,khd->hqk", grad_att, values, preferred_element_type=jnp.float32
        )
        grad_scores = weights * (
            grad_weights - jnp.sum(weights * grad_weights, axis=-1, keepdims=True)
        )
        grad_scores = grad_scores.astype(jnp.bfloat16)
        scaling = query_rows.shape[2] ** (-0.5)
        grad_query = (
            jnp.einsum("hqk,khd->qhd", grad_scores, key_rows, preferred_element_type=jnp.float32)
            * scaling
        )
        grad_keys = (
            jnp.einsum("hqk,qhd->khd", grad_scores, query_rows, preferred_element_type=jnp.float32)
            * scaling
        )
        return jnp.stack(
            (
                grad_query.astype(jnp.bfloat16),
                grad_keys.astype(jnp.bfloat16),
                grad_values.astype(jnp.bfloat16),
            ),
            axis=1,
        )

    proj_full, up_full = fetch_inner(projection, up_weight)
    out_full, down_full = fetch_outer(out_weight, down_weight)
    model_width = proj_full.shape[0]
    flat_proj = proj_full.reshape(model_width, 3 * slab_width)
    x_float = inputs.astype(jnp.float32)
    normed_one, inverse_one = normalize(x_float)
    rows_one = gather_normed((normed_one * gain_one + shift_one).astype(jnp.bfloat16))
    projected = jnp.dot(rows_one, flat_proj, preferred_element_type=jnp.float32).reshape(
        group_rows, 3, slab_width
    )
    queries = (projected[:, 0] + query_bias).astype(jnp.bfloat16)
    key_rows = projected[:, 1].astype(jnp.bfloat16)
    values = (projected[:, 2] + value_bias).astype(jnp.bfloat16)
    attended, log_total = lax.map(
        forward_one, (by_sequence(queries), by_sequence(key_rows), by_sequence(values), lengths)
    )
    attended = attended.reshape(group_rows, slab_width)
    branch = branch_sum(attended, out_full) + out_bias
    middle = x_float + live_rows * branch
    normed_two, inverse_two = normalize(middle)
    rows_two = gather_normed((normed_two * gain_two + shift_two).astype(jnp.bfloat16))
    before = jnp.dot(rows_two, up_full, preferred_element_type=jnp.float32) + up_bias
    active = jax.nn.gelu(before, approximate=False).astype(jnp.bfloat16)
    dense_out = branch_sum(active, down_full) + down_bias
    output = (middle + live_rows * dense_out).astype(jnp.bfloat16)
    proj_full, up_full = fetch_inner(projection, up_weight)
    out_full, down_full = fetch_outer(out_weight, down_weight)
    flat_proj = proj_full.reshape(model_width, 3 * slab_width)
    grad_out = cotangent.astype(jnp.float32)
    grad_dense = (live_rows * grad_out).astype(jnp.bfloat16)
    rows_dense = gather_grads(grad_dense)
    down_grad = outer_sum(active, rows_dense)
    grad_active = against(rows_dense, down_full)
    grad_before = (grad_active * gelu_slope(before)).astype(jnp.bfloat16)
    up_grad = outer_sum(rows_two, grad_before)
    grad_two = input_sum(grad_before, up_full)
    gain_two_part = jnp.sum(grad_two * normed_two, axis=0)
    shift_two_part = jnp.sum(grad_two, axis=0)
    grad_middle = grad_out + norm_back(grad_two, normed_two, inverse_two, gain_two)
    grad_branch = (live_rows * grad_middle).astype(jnp.bfloat16)
    rows_branch = gather_grads(grad_branch)
    out_grad = outer_sum(attended, rows_branch)
    grad_attended = against(rows_branch, out_full).astype(jnp.bfloat16)
    stacked = lax.map(
        backward_one,
        (
            by_sequence(queries),
            by_sequence(key_rows),
            by_sequence(values),
            lengths,
            log_total,
            by_sequence(grad_attended),
        ),
    )
    flat_grad = stacked.reshape(group_rows, 3 * slab_width)
    proj_grad = outer_sum(rows_one, flat_grad).reshape(model_width, 3, slab_width)
    grad_one = input_sum(flat_grad, flat_proj)
    gain_one_part = jnp.sum(grad_one * normed_one, axis=0)
    shift_one_part = jnp.sum(grad_one, axis=0)
    inputs_grad = grad_middle + norm_back(grad_one, normed_one, inverse_one, gain_one)
    proj_part, up_part = (
        lax.psum_scatter(
            proj_grad.astype(jnp.bfloat16), "rows", scatter_dimension=0, tiled=True
        ).astype(jnp.float32),
        lax.psum_scatter(
            up_grad.astype(jnp.bfloat16), "rows", scatter_dimension=0, tiled=True
        ).astype(jnp.float32),
    )
    out_part, down_part = (
        lax.psum_scatter(
            out_grad.astype(jnp.bfloat16), "rows", scatter_dimension=1, tiled=True
        ).astype(jnp.float32),
        lax.psum_scatter(
            down_grad.astype(jnp.bfloat16), "rows", scatter_dimension=1, tiled=True
        ).astype(jnp.float32),
    )
    bias_terms = jnp.sum(flat_grad.reshape(group_rows, 3, slab_width), axis=0, dtype=jnp.float32)
    up_bias_part = jnp.sum(grad_before, axis=0, dtype=jnp.float32)
    query_total, value_total, up_bias_total = lax.psum(
        (bias_terms[0], bias_terms[2], up_bias_part), "rows"
    )
    out_bias_part = jnp.sum(grad_branch, axis=0, dtype=jnp.float32)
    down_bias_part = jnp.sum(grad_dense, axis=0, dtype=jnp.float32)
    (
        gain_one_total,
        shift_one_total,
        gain_two_total,
        shift_two_total,
        out_bias_total,
        down_bias_total,
    ) = lax.psum(
        (
            gain_one_part,
            shift_one_part,
            gain_two_part,
            shift_two_part,
            out_bias_part,
            down_bias_part,
        ),
        ("rows", "cols"),
    )
    return (
        output,
        inputs_grad,
        gain_one_total,
        shift_one_total,
        proj_part,
        query_total,
        value_total,
        out_part,
        out_bias_total,
        gain_two_total,
        shift_two_total,
        up_part,
        up_bias_total,
        down_part,
        down_bias_total,
    )


def solution(mesh):
    placed = (
        P(("rows", "cols"), None),
        P("rows"),
        P(),
        P(),
        P("rows", None, "cols"),
        P("cols"),
        P("cols"),
        P("cols", "rows"),
        P(),
        P(),
        P(),
        P("rows", "cols"),
        P("cols"),
        P("cols", "rows"),
        P(),
        P(("rows", "cols"), None),
    )
    return jax.shard_map(
        per_device,
        mesh=mesh,
        in_specs=placed,
        out_specs=(
            P(("rows", "cols"), None),
            P(("rows", "cols"), None),
            P(),
            P(),
            P("rows", None, "cols"),
            P("cols"),
            P("cols"),
            P("cols", "rows"),
            P(),
            P(),
            P(),
            P("rows", "cols"),
            P("cols"),
            P("cols", "rows"),
            P(),
        ),
        check_vma=False,
    )
```

profile of v0, /device:TPU:0, one launch (start us, length us, event | category | flops | bytes accessed | tf_op | source)
XLA Modules:
  0.0 1182.6 jit_solution(13567577021857302794)
XLA Ops:
  10.4 2.7 fusion.38
  15.2 2.7 subtract_convert_fusion
  19.0 77.7 %all-gather.9.cloned.1.call-done = bf16[1024,2048]{1,0:T(8,128)(2,1)} async-done(((bf16[256,2048]{1,0:T(8,128)(2,1)}), bf16[1024,2048]{1,0:T(8,128)(2,1)}) %all-gather.9.cloned.1.call-update) | async-done | bytes 4194320 | tf_op jit(solution)/shard_map/all_gather | solution.py:75
  96.7 47.7 %all-gather.11.cloned.1.call-done = bf16[2048,3,512]{0,2,1:T(8,128)(2,1)} async-done(((bf16[256,3,512]{0,2,1:T(8,128)(2,1)}), bf16[2048,3,512]{0,2,1:T(8,128)(2,1)}) %all-gather.11.cloned.1.call-update) | async-done | bytes 6291472 | tf_op jit(solution)/shard_map/all_gather | solution.py:62
  144.4 10.3 fusion.22
  155.9 18.5 %fusion.59 = (f32[8,1024]{1,0:T(8,128)S(1)}, f32[8,1024,1024]{1,2,0:T(8,128)}) fusion(f32[1024,1024]{0,1:T(8,128)} %subtract_convert_fusion, f32[8]{0:T(128)S(1)} %multiply_exponential_fusion, bf16[1024,8,64]{0,2,1:T(8,128)(2,1)S(1)} %bitcast.84, f32[1024,8,64]{0,2,1:T(8,128)S(1)} %bitcast.80, f32[8,64]{1,0:T(8,128)S(1)} %add.205, ...), kind=kOutput, calls=%fused_computation.126 | convolution fusion | flops 1116725248 | bytes 41977888 | tf_op jit(solution)/shard_map/while/body/eval_jaxpr/qhd,khd->hqk/dot_general | solution.py:52
  174.4 13.1 %fusion = f32[8,1024]{1,0:T(8,128)S(1)} fusion(f32[8,1024,1024]{1,2,0:T(8,128)} %get-tuple-element.95, f32[8,1024]{1,0:T(8,128)S(1)} %get-tuple-element.94), kind=kLoop, calls=%fused_computation.6 | loop fusion | flops 16769024 | bytes 33619968 | tf_op jit(solution)/shard_map/while/body/eval_jaxpr/reduce_sum | solution.py:139
  187.5 14.3 %fusion.53 = bf16[8,64,1024]{2,1,0:T(8,128)(2,1)S(1)} fusion(f32[8,1024,1024]{1,2,0:T(8,128)} %get-tuple-element.95, f32[8,1024]{1,0:T(8,128)S(1)} %fusion, f32[8,1024]{1,0:T(8,128)S(1)} %get-tuple-element.94, f32[1024,8,64]{0,2,1:T(8,128)S(1)} %bitcast.78, f32[8,64]{1,0:T(8,128)S(1)} %add.202), kind=kOutput, calls=%fused_computation.103 | convolution fusion | flops 1100480512 | bytes 36767744 | tf_op jit(solution)/shard_map/while/body/eval_jaxpr/hqk,khd->qhd/dot_general | solution.py:141
  201.8 6.3 convolution_convert_fusion.6
  208.8 76.3 %reduce-scatter.9.cloned.1.call-done = bf16[256,2048]{1,0:T(8,128)(2,1)} async-done(((bf16[1024,2048]{1,0:T(8,128)(2,1)}), bf16[256,2048]{1,0:T(8,128)(2,1)}) %reduce-scatter.9.cloned.1.call-update) | async-done | bytes 1048592 | tf_op jit(solution)/shard_map/reduce_scatter | solution.py:83
  287.0 1.9 multiply_reduce_fusion.1
  289.0 2.7 convert_reduce_fusion.5
  293.3 48.7 %all-gather.17.cloned.1.call-done = bf16[2048,2048]{1,0:T(8,128)(2,1)} async-done(((bf16[256,2048]{1,0:T(8,128)(2,1)}), bf16[2048,2048]{1,0:T(8,128)(2,1)}) %all-gather.17.cloned.1.call-update) | async-done | bytes 8388624 | tf_op jit(solution)/shard_map/all_gather | solution.py:63
  342.0 82.9 %all-gather.15.cloned.1.call-done = bf16[1024,2048]{1,0:T(8,128)(2,1)} async-done(((bf16[256,2048]{1,0:T(8,128)(2,1)}), bf16[1024,2048]{1,0:T(8,128)(2,1)}) %all-gather.15.cloned.1.call-update) | async-done | bytes 4194320 | tf_op jit(solution)/shard_map/all_gather | solution.py:75
  424.9 30.9 %fusion.8 = (bf16[1024,2048]{1,0:T(8,128)(2,1)}, f32[1024,2048]{1,0:T(8,128)}) fusion(f32[2048]{0:T(1024)S(1)} %copy-done.36, bf16[1024,2048]{1,0:T(8,128)(2,1)} %all-gather.15.cloned.1.call-done, bf16[2048,2048]{1,0:T(8,128)(2,1)} %all-gather.17.cloned.1.call-done), kind=kOutput, calls=%fused_computation.15 | convolution fusion | flops 8728346624 | bytes 25174016 | tf_op jit(solution)/shard_map/dot_general | solution.py:198
  455.7 25.7 %all-gather.19.cloned.1.call-done = bf16[2048,2048]{1,0:T(8,128)(2,1)} async-done(((bf16[2048,256]{1,0:T(8,128)(2,1)}), bf16[2048,2048]{1,0:T(8,128)(2,1)}) %all-gather.19.cloned.1.call-update) | async-done | bytes 8388624 | tf_op jit(solution)/shard_map/all_gather | solution.py:70
  481.4 83.0 %all-gather.21.cloned.1.call-done = bf16[1024,2048]{1,0:T(8,128)(2,1)} async-done(((bf16[256,2048]{1,0:T(8,128)(2,1)}), bf16[1024,2048]{1,0:T(8,128)(2,1)}) %all-gather.21.cloned.1.call-update) | async-done | bytes 4194320 | tf_op jit(solution)/shard_map/all_gather | solution.py:79
  564.4 17.0 %convert_reduce_fusion = (f32[2048]{0:T(1024)}, bf16[1024,2048]{1,0:T(8,128)(2,1)S(1)}) fusion(f32[1024,2048]{1,0:T(8,128)} %get-tuple-element.97, f32[2048]{0:T(1024)S(1)} %copy-done.36, bf16[1024,2048]{1,0:T(8,128)(2,1)} %all-gather.21.cloned.1.call-done, bf16[2048,2048]{1,0:T(8,128)(2,1)} %all-gather.19.cloned.1.call-done), kind=kOutput, calls=%fused_computation.22 | convolution fusion | flops 8617195520 | bytes 25182208 | tf_op jit(solution)/shard_map/dot_general | solution.py:31
  581.4 2.1 copy-done.38
  583.5 10.6 convolution_convert_fusion.4
  594.2 13.9 %convolution_convert_fusion.5 = bf16[1024,2048]{1,0:T(8,128)(2,1)} fusion(bf16[1024,2048]{1,0:T(8,128)(2,1)} %get-tuple-element.96, bf16[2048,2048]{1,0:T(8,128)(2,1)} %all-gather.19.cloned.1.call-done), kind=kOutput, calls=%fused_computation.51 | convolution fusion | flops 8592031744 | bytes 16777216 | tf_op jit(solution)/shard_map/dot_general | solution.py:84
  608.2 61.4 %reduce-scatter.13.cloned.1.call-done = bf16[256,2048]{1,0:T(8,128)(2,1)} async-done(((bf16[1024,2048]{1,0:T(8,128)(2,1)}), bf16[256,2048]{1,0:T(8,128)(2,1)}) %reduce-scatter.13.cloned.1.call-update) | async-done | bytes 1048592 | tf_op jit(solution)/shard_map/reduce_scatter | solution.py:92
  669.6 2.6 fusion.48
  672.2 76.8 %reduce-scatter.11.cloned.1.call-done = bf16[256,2048]{1,0:T(8,128)(2,1)} async-done(((bf16[1024,2048]{1,0:T(8,128)(2,1)}), bf16[256,2048]{1,0:T(8,128)(2,1)}) %reduce-scatter.11.cloned.1.call-update) | async-done | bytes 1048592 | tf_op jit(solution)/shard_map/reduce_scatter | solution.py:83
  749.0 4.4 convert_reduce_fusion.6
  753.5 14.3 %convolution_convert_fusion = bf16[2048,2048]{1,0:T(8,128)(2,1)} fusion(bf16[1024,2048]{1,0:T(8,128)(2,1)} %get-tuple-element.96, bf16[1024,2048]{1,0:T(8,128)(2,1)} %all-gather.21.cloned.1.call-done), kind=kOutput, calls=%fused_computation.38 | convolution fusion | flops 8594128896 | bytes 16777216 | tf_op jit(solution)/shard_map/dot_general | solution.py:37
  767.9 14.1 %convolution_convert_fusion.1 = bf16[2048,2048]{1,0:T(8,128)(2,1)} fusion(bf16[1024,2048]{1,0:T(8,128)(2,1)} %all-gather.15.cloned.1.call-done, bf16[1024,2048]{1,0:T(8,128)(2,1)} %copy-done.38), kind=kOutput, calls=%fused_computation.39 | convolution fusion | flops 8594128896 | bytes 16777216 | tf_op jit(solution)/shard_map/dot_general | solution.py:37
  782.7 52.1 %all-gather.23.cloned.1.call-done = bf16[1024,2048]{1,0:T(8,128)(2,1)} async-done(((bf16[256,2048]{1,0:T(8,128)(2,1)}), bf16[1024,2048]{1,0:T(8,128)(2,1)}) %all-gather.23.cloned.1.call-update) | async-done | bytes 4194320 | tf_op jit(solution)/shard_map/all_gather | solution.py:79
  834.9 6.2 convolution_convert_fusion.7
  841.0 5.4 convolution_convert_fusion.8
  846.5 25.0 %multiply_reduce_fusion = (f32[8,1024]{1,0:T(8,128)S(1)}, f32[8,1024,1024]{1,2,0:T(8,128)}) fusion(f32[8,1024,1024]{1,2,0:T(8,128)} %get-tuple-element.95, f32[8,1024]{1,0:T(8,128)S(1)} %log_add_fusion, bf16[1024,8,64]{0,2,1:T(8,128)(2,1)S(1)} %bitcast.82, f32[1024,8,64]{0,2,1:T(8,128)S(1)} %bitcast.79, f32[8,64]{1,0:T(8,128)S(1)} %copy-done.19), kind=kOutput, calls=%fused_computation.1 | convolution fusion | flops 1099948032 | bytes 70322176 | tf_op jit(solution)/shard_map/while/body/eval_jaxpr/qhd,khd->hqk/dot_general | solution.py:152
  871.5 29.8 %multiply_convert_fusion = bf16[8,1024,1024]{1,2,0:T(8,128)(2,1)} fusion(f32[8,1024,1024]{1,2,0:T(8,128)} %get-tuple-element.99, f32[8,1024,1024]{1,2,0:T(8,128)} %get-tuple-element.95, f32[8,1024]{1,0:T(8,128)S(1)} %get-tuple-element.98, f32[8,1024]{1,0:T(8,128)S(1)} %log_add_fusion), kind=kLoop, calls=%fused_computation | loop fusion | flops 33554432 | bytes 83951616 | tf_op jit(solution)/shard_map/while/body/eval_jaxpr/convert_element_type | solution.py:158
  901.3 12.2 %multiply_convert_fusion.1 = bf16[8,64,1024]{2,1,0:T(8,128)(2,1)} fusion(bf16[8,1024,1024]{1,2,0:T(8,128)(2,1)} %multiply_convert_fusion, f32[1024,8,64]{0,2,1:T(8,128)S(1)} %bitcast.81, f32[8,64]{1,0:T(8,128)S(1)} %copy-done.28), kind=kOutput, calls=%fused_computation.92 | convolution fusion | flops 1075838976 | bytes 19924992 | tf_op jit(solution)/shard_map/while/body/eval_jaxpr/hqk,qhd->khd/dot_general | solution.py:165
  913.5 17.6 %fusion.50 = bf16[8,64,1024]{2,1,0:T(8,128)(2,1)S(1)} fusion(bf16[1024,8,64]{0,2,1:T(8,128)(2,1)} %bitcast.83, f32[8,1024,1024]{1,2,0:T(8,128)} %get-tuple-element.95, f32[8,1024]{1,0:T(8,128)S(1)} %log_add_fusion), kind=kOutput, calls=%fused_computation.101 | convolution fusion | flops 1091043328 | bytes 35684352 | tf_op jit(solution)/shard_map/while/body/eval_jaxpr/hqk,qhd->khd/dot_general | solution.py:149
  931.2 9.5 multiply_convert_fusion.2
  942.8 11.7 convolution_convert_fusion.3
  954.5 11.6 convolution_convert_fusion.2
  966.1 2.7 convert_element_type.212
  968.8 14.3 %reduce-scatter.21.cloned.1.call-done = bf16[256,2048]{1,0:T(8,128)(2,1)} async-done(((bf16[2048,2048]{1,0:T(8,128)(2,1)}), bf16[256,2048]{1,0:T(8,128)(2,1)}) %reduce-scatter.21.cloned.1.call-update) | async-done | bytes 1048592 | tf_op jit(solution)/shard_map/reduce_scatter | solution.py:241
  983.2 2.8 convert_element_type.209
  987.7 23.3 %all-reduce.1 = (f32[512]{0:T(512)}, f32[512]{0:T(512)}, f32[2048]{0:T(1024)}) all-reduce(f32[512]{0:T(512)S(1)} %bitcast.89, f32[512]{0:T(512)S(1)} %bitcast.88, f32[2048]{0:T(1024)S(1)} %copy-done.31), channel_id=1, replica_groups=mesh['rows'=8,'cols'=4] {'rows'}, use_global_device_ids=true, to_apply=%region_21.22 | all-reduce | flops 3072 | bytes 24576 | tf_op jit(solution)/shard_map/psum | solution.py:255
  1011.0 16.9 %reduce-scatter.19.cloned.1.call-done = bf16[512,256]{1,0:T(8,128)(2,1)} async-done(((bf16[512,2048]{1,0:T(8,128)(2,1)}), bf16[512,256]{1,0:T(8,128)(2,1)}) %reduce-scatter.19.cloned.1.call-update) | async-done | bytes 262160 | tf_op jit(solution)/shard_map/reduce_scatter | solution.py:246
  1029.7 77.2 %reduce-scatter.15.cloned.1.call-done = bf16[256,2048]{1,0:T(8,128)(2,1)} async-done(((bf16[1024,2048]{1,0:T(8,128)(2,1)}), bf16[256,2048]{1,0:T(8,128)(2,1)}) %reduce-scatter.15.cloned.1.call-update) | async-done | bytes 1048592 | tf_op jit(solution)/shard_map/reduce_scatter | solution.py:92
  1106.9 2.3 fusion.49
  1109.1 42.3 %all-reduce = (f32[2048]{0:T(1024)}, f32[2048]{0:T(1024)}, f32[2048]{0:T(1024)}, f32[2048]{0:T(1024)}, f32[2048]{0:T(1024)}, /*index=5*/f32[2048]{0:T(1024)}) all-reduce(f32[2048]{0:T(1024)S(1)} %get-tuple-element.68, f32[2048]{0:T(1024)S(1)} %get-tuple-element.73, ...), channel_id=1, replica_groups=mesh['rows'=8,'cols'=4] {'rows','cols'}, use_global_device_ids=true, to_apply=%region_16.17 | all-reduce | flops 12288 | bytes 98304 | tf_op jit(solution)/shard_map/psum | solution.py:267
  1151.4 3.4 fusion.41
  1154.8 18.6 %reduce-scatter.17.cloned.1.call-done = bf16[256,3,512]{2,0,1:T(8,128)(2,1)} async-done(((bf16[2048,3,512]{2,0,1:T(8,128)(2,1)}), bf16[256,3,512]{2,0,1:T(8,128)(2,1)}) %reduce-scatter.17.cloned.1.call-update) | async-done | bytes 786448 | tf_op jit(solution)/shard_map/reduce_scatter | solution.py:238
  1173.4 2.5 convert_element_type.203
  (135 shorter events, 17.8 us)
Async XLA Ops:
  7.2 6.0 copy-start.12
  7.2 89.6 %all-gather.9.cloned.1.call-start = ((), (), s32[]{:S(2)}) async-start(), calls=%async_computation.8 | async-start | bytes 5242880 | tf_op jit(solution)/shard_map/all_gather | solution.py:75
  8.8 9.1 copy-start.23
  10.4 7.4 copy-start.25
  13.1 5.4 copy-start.32
  13.1 5.5 copy-start.33
  13.1 131.3 %all-gather.11.cloned.1.call-start = ((), (), s32[]{:S(2)}) async-start(), calls=%async_computation.9 | async-start | bytes 7077888 | tf_op jit(solution)/shard_map/all_gather | solution.py:62
  14.4 187.4 %all-gather.13.cloned.1.call-start = ((), (), s32[]{:S(2)}) async-start(), calls=%async_computation.10 | async-start | bytes 2359296 | tf_op jit(solution)/shard_map/all_gather | solution.py:69
  15.1 270.1 %reduce-scatter.9.cloned.1.call-start = ((), (), s32[]{:S(2)}) async-start(), calls=%async_computation.11 | async-start | bytes 5242880 | tf_op jit(solution)/shard_map/reduce_scatter | solution.py:83
  18.6 136.6 %copy-start.27 = (f32[8,64]{1,0:T(8,128)}, f32[8,64]{1,0:T(8,128)S(1)}, u32[]{:S(2)}) copy-start(f32[8,64]{1,0:T(8,128)S(1)} %add.205) | copy-start | bytes 6148
  18.7 168.8 %copy-start.18 = (f32[8,64]{1,0:T(8,128)}, f32[8,64]{1,0:T(8,128)S(1)}, u32[]{:S(2)}) copy-start(f32[8,64]{1,0:T(8,128)S(1)} %add.202) | copy-start | bytes 6148
  155.2 19.2 %copy-start.6 = (f32[1024,1,512]{0,2,1:T(8,128)}, f32[1024,1,512]{0,2,1:T(8,128)S(1)}, u32[]{:S(2)}) copy-start(f32[1024,1,512]{0,2,1:T(8,128)S(1)} %get-tuple-element.89) | copy-start | bytes 6291460
  155.2 32.3 %copy-start.3 = (f32[1024,1,512]{0,2,1:T(8,128)}, f32[1024,1,512]{0,2,1:T(8,128)S(1)}, u32[]{:S(2)}) copy-start(f32[1024,1,512]{0,2,1:T(8,128)S(1)} %get-tuple-element.88) | copy-start | bytes 6291460
  174.4 13.1 %copy-start.14 = (f32[8,1024]{1,0:T(8,128)}, f32[8,1024]{1,0:T(8,128)S(1)}, u32[]{:S(2)}) copy-start(f32[8,1024]{1,0:T(8,128)S(1)} %get-tuple-element.94) | copy-start | bytes 98308
  187.5 14.3 %copy-start.16 = (f32[8,1024]{1,0:T(8,128)}, f32[8,1024]{1,0:T(8,128)S(1)}, u32[]{:S(2)}) copy-start(f32[8,1024]{1,0:T(8,128)S(1)} %fusion) | copy-start | bytes 98308
  201.8 6.3 copy-start.37
  208.1 77.1 %copy-start = (bf16[256,2048]{1,0:T(8,128)(2,1)S(1)}, bf16[256,2048]{1,0:T(8,128)(2,1)}, u32[]{:S(2)}) copy-start(bf16[256,2048]{1,0:T(8,128)(2,1)} %param.16) | copy-start | bytes 3145732
  208.1 77.1 %copy-start.13 = (f32[2048]{0:T(1024)S(1)}, f32[2048]{0:T(1024)}, u32[]{:S(2)}) copy-start(f32[2048]{0:T(1024)} %param.24) | copy-start | bytes 24580
  208.1 80.8 %copy-start.10 = (bf16[256,2048]{1,0:T(8,128)(2,1)S(1)}, bf16[256,2048]{1,0:T(8,128)(2,1)}, u32[]{:S(2)}) copy-start(bf16[256,2048]{1,0:T(8,128)(2,1)} %param.31) | copy-start | bytes 3145732
  208.1 80.8 %copy-start.20 = (f32[2048]{0:T(1024)S(1)}, f32[2048]{0:T(1024)}, u32[]{:S(2)}) copy-start(f32[2048]{0:T(1024)} %param.25) | copy-start | bytes 24580
  208.1 80.8 %copy-start.29 = (f32[2048]{0:T(1024)S(1)}, f32[2048]{0:T(1024)}, u32[]{:S(2)}) copy-start(f32[2048]{0:T(1024)} %param.26) | copy-start | bytes 24580
  208.2 133.8 %all-gather.17.cloned.1.call-start = ((), (), s32[]{:S(2)}) async-start(), calls=%async_computation.13 | async-start | bytes 9437184 | tf_op jit(solution)/shard_map/all_gather | solution.py:63
  208.7 216.1 %all-gather.15.cloned.1.call-start = ((), (), s32[]{:S(2)}) async-start(), calls=%async_computation.12 | async-start | bytes 5242880 | tf_op jit(solution)/shard_map/all_gather | solution.py:75
  289.0 135.9 %copy-start.36 = (f32[2048]{0:T(1024)S(1)}, f32[2048]{0:T(1024)}, u32[]{:S(2)}) copy-start(f32[2048]{0:T(1024)} %param.28) | copy-start | bytes 24580
  291.7 189.7 %all-gather.19.cloned.1.call-start = ((), (), s32[]{:S(2)}) async-start(), calls=%async_computation.14 | async-start | bytes 9437184 | tf_op jit(solution)/shard_map/all_gather | solution.py:70
  292.5 272.0 %all-gather.21.cloned.1.call-start = ((), (), s32[]{:S(2)}) async-start(), calls=%async_computation.16 | async-start | bytes 5242880 | tf_op jit(solution)/shard_map/all_gather | solution.py:79
  293.2 376.4 %reduce-scatter.13.cloned.1.call-start = ((), (), s32[]{:S(2)}) async-start(), calls=%async_computation.17 | async-start | bytes 5242880 | tf_op jit(solution)/shard_map/reduce_scatter | solution.py:92
  564.4 19.1 %copy-start.34 = (bf16[2048,2048]{1,0:T(8,128)(2,1)S(1)}, bf16[2048,2048]{1,0:T(8,128)(2,1)}, u32[]{:S(2)}) copy-start(bf16[2048,2048]{1,0:T(8,128)(2,1)} %all-gather.17.cloned.1.call-done) | copy-start | bytes 25165828
  594.1 154.9 %reduce-scatter.11.cloned.1.call-start = ((), (), s32[]{:S(2)}) async-start(), calls=%async_computation.15 | async-start | bytes 5242880 | tf_op jit(solution)/shard_map/reduce_scatter | solution.py:83
  608.1 140.9 %copy-start.30 = (f32[2048]{0:T(1024)S(1)}, f32[2048]{0:T(1024)}, u32[]{:S(2)}) copy-start(f32[2048]{0:T(1024)} %param.30) | copy-start | bytes 24580
  608.1 226.7 %all-gather.23.cloned.1.call-start = ((), (), s32[]{:S(2)}) async-start(), calls=%async_computation.18 | async-start | bytes 5242880 | tf_op jit(solution)/shard_map/all_gather | solution.py:79
  753.4 212.7 %reduce-scatter.23.cloned.1.call-start = ((), (), s32[]{:S(2)}) async-start(), calls=%async_computation.23 | async-start | bytes 9437184 | tf_op jit(solution)/shard_map/reduce_scatter | solution.py:249
  767.8 215.4 %reduce-scatter.21.cloned.1.call-start = ((), (), s32[]{:S(2)}) async-start(), calls=%async_computation.22 | async-start | bytes 9437184 | tf_op jit(solution)/shard_map/reduce_scatter | solution.py:241
  781.9 246.0 %reduce-scatter.19.cloned.1.call-start = ((), (), s32[]{:S(2)}) async-start(), calls=%async_computation.21 | async-start | bytes 2359296 | tf_op jit(solution)/shard_map/reduce_scatter | solution.py:246
  782.7 58.3 %copy-start.35 = (bf16[512,2048]{1,0:T(8,128)(2,1)S(1)}, bf16[512,2048]{1,0:T(8,128)(2,1)}, u32[]{:S(2)}) copy-start(bf16[512,2048]{1,0:T(8,128)(2,1)} %all-gather.13.cloned.1.call-done) | copy-start | bytes 6291460
  841.0 5.4 copy-start.19
  846.4 25.1 %copy-start.8 = (bf16[1024,512]{0,1:T(8,128)(2,1)}, bf16[1024,512]{0,1:T(8,128)(2,1)S(1)}, u32[]{:S(2)}) copy-start(bf16[1024,512]{0,1:T(8,128)(2,1)S(1)} %convolution_convert_fusion.8) | copy-start | bytes 3145732
  871.5 29.8 %copy-start.7 = (f32[1024,1,512]{0,2,1:T(8,128)S(1)}, f32[1024,1,512]{0,2,1:T(8,128)}, u32[]{:S(2)}) copy-start(f32[1024,1,512]{0,2,1:T(8,128)} %copy-done.6) | copy-start | bytes 6291460
  871.5 29.8 %copy-start.28 = (f32[8,64]{1,0:T(8,128)S(1)}, f32[8,64]{1,0:T(8,128)}, u32[]{:S(2)}) copy-start(f32[8,64]{1,0:T(8,128)} %copy-done.27) | copy-start | bytes 6148
  931.1 175.8 %reduce-scatter.15.cloned.1.call-start = ((), (), s32[]{:S(2)}) async-start(), calls=%async_computation.19 | async-start | bytes 5242880 | tf_op jit(solution)/shard_map/reduce_scatter | solution.py:92
  931.2 9.5 copy-start.2
  954.4 218.9 %reduce-scatter.17.cloned.1.call-start = ((), (), s32[]{:S(2)}) async-start(), calls=%async_computation.20 | async-start | bytes 7077888 | tf_op jit(solution)/shard_map/reduce_scatter | solution.py:238
  966.1 21.6 %copy-start.31 = (f32[2048]{0:T(1024)S(1)}, f32[2048]{0:T(1024)}, u32[]{:S(2)}) copy-start(f32[2048]{0:T(1024)} %get-tuple-element.100) | copy-start | bytes 24580
  968.8 138.0 %copy-start.21 = (f32[2048]{0:T(1024)S(1)}, f32[2048]{0:T(1024)}, u32[]{:S(2)}) copy-start(f32[2048]{0:T(1024)} %param.18) | copy-start | bytes 24580
  968.8 138.0 %copy-start.24 = (f32[256]{0:T(256)S(1)}, f32[256]{0:T(256)}, u32[]{:S(2)}) copy-start(f32[256]{0:T(256)} %copy-done.23) | copy-start | bytes 3076
  968.8 138.0 %copy-start.26 = (f32[256]{0:T(256)S(1)}, f32[256]{0:T(256)}, u32[]{:S(2)}) copy-start(f32[256]{0:T(256)} %copy-done.25) | copy-start | bytes 3076
  968.8 140.3 %copy-start.22 = (f32[2048]{0:T(1024)S(1)}, f32[2048]{0:T(1024)}, u32[]{:S(2)}) copy-start(f32[2048]{0:T(1024)} %get-tuple-element.83) | copy-start | bytes 24580
  987.7 163.7 %copy-start.5 = (f32[256,2048]{1,0:T(8,128)S(1)}, f32[256,2048]{1,0:T(8,128)}, u32[]{:S(2)}) copy-start(f32[256,2048]{1,0:T(8,128)} %get-tuple-element.87) | copy-start | bytes 6291460
  (7 other events, 15.5 us)
Sparse Core Ops, SparseCore 0:
  13.2 83.4 all-gather.8
  99.2 45.1 all-gather.10
  146.3 28.1 all-gather.12
  208.3 76.8 reduce-scatter.8
  287.1 54.8 all-gather.16
  344.1 80.7 all-gather.14
  426.9 54.4 all-gather.18
  483.6 80.7 all-gather.20
  594.3 75.2 reduce-scatter.12
  671.7 77.2 reduce-scatter.10
  753.6 81.2 all-gather.22
  838.6 69.8 reduce-scatter.22
  911.9 71.2 reduce-scatter.20
  986.7 41.1 reduce-scatter.18
  1030.0 76.7 reduce-scatter.14
  1110.5 62.8 reduce-scatter.16
where the time goes:
time: 1190 us; the launch traced here: 1180 us
  waiting for transfers between devices  762 us (64%)
  matrix products  249 us (21%)
  other arithmetic  82.7 us (7%)
  blocking collectives  65.6 us (6%)
  between operations  15.3 us (1%)
    all_gather x2, waiting for transfers between devices, gather_normed(): return lax.all_gather(rows_local, 'cols', axis=0, tiled=True)  161 us
    reduce_scatter x2, waiting for transfers between devices, branch_sum(): lax.psum_scatter(jnp.dot(source, weight, preferred_element_type=jnp.float...  153 us
    reduce_scatter x2, waiting for transfers between devices, input_sum(): lax.psum_scatter(against(source, weight).astype(jnp.bfloat16), 'cols', sc...  139 us
    all_gather x2, waiting for transfers between devices, gather_grads(): return lax.all_gather(rows_local, 'cols', axis=0, tiled=True)  135 us
    all_gather x1, waiting for transfers between devices, fetch_inner(): lax.all_gather(up_weight, 'rows', axis=0, tiled=True)  48.7 us
    all_gather x1, waiting for transfers between devices, fetch_inner(): lax.all_gather(projection, 'rows', axis=0, tiled=True)  47.7 us
    dot_general x4, matrix products, outer_sum(): lax.dot_general(left_rows, right_rows, (((0,), (0,)), ((), ())), preferre...  46.1 us
    dot_general x4, matrix products, against(): lax.dot_general(left_rows, right_rows, (((1,), (1,)), ((), ())), preferre...  44.7 us
  transfers between devices with their start and end apart: 16, of which 14 were waited for; matrix products, arithmetic and copies ran while one was open for 24% of the time, Pallas kernels for 0%

commit v1 on v0

v1 whole, which is shorter than its diff:
```python
import functools
import math

import jax
import jax.numpy as jnp
from jax import lax
from jax.experimental import pallas as pl
from jax.experimental.pallas import tpu as pltpu
from jax.sharding import PartitionSpec as P

HEADS = 32
HEAD_DIM = 64
LOG2E = 1.4426950408889634
LOW = -1.0e9
epsilon = 1e-05
bf16 = jnp.bfloat16
f32 = jnp.float32
MESH = pl.DeviceIdType.MESH
VM = pl.BlockSpec(memory_space=pltpu.VMEM)
SM = pl.BlockSpec(memory_space=pltpu.SMEM)
HB = pl.BlockSpec(memory_space=pl.ANY)


def nn(a, b):
    return lax.dot_general(a, b, (((1,), (0,)), ((), ())), preferred_element_type=f32)


def nt(a, b):
    return lax.dot_general(a, b, (((1,), (1,)), ((), ())), preferred_element_type=f32)


def tn(a, b):
    return lax.dot_general(a, b, (((0,), (0,)), ((), ())), preferred_element_type=f32)


def normalize(values):
    center = jnp.mean(values, axis=-1, keepdims=True)
    centred = values - center
    spread = jnp.mean(centred * centred, axis=-1, keepdims=True)
    inverse = lax.rsqrt(spread + epsilon)
    return centred * inverse, inverse


def norm_back(grad_rows, normed, inverse, gain_row):
    scaled = grad_rows * gain_row
    first_mean = jnp.mean(scaled, axis=-1, keepdims=True)
    second = jnp.mean(scaled * normed, axis=-1, keepdims=True)
    return inverse * (scaled - first_mean - normed * second)


def live_mask(length, start, rows):
    return (start + lax.broadcasted_iota(jnp.int32, (rows, 1), 0) < length).astype(f32)


def line_barrier(r, c, n):
    barrier = pltpu.get_barrier_semaphore()

    @pl.when(c > 0)
    def _():
        pl.semaphore_signal(barrier, inc=1, device_id=(r, c - 1), device_id_type=MESH)

    @pl.when(c < n - 1)
    def _():
        pl.semaphore_signal(barrier, inc=1, device_id=(r, c + 1), device_id_type=MESH)

    pl.semaphore_wait(barrier, (c > 0).astype(jnp.int32) + (c < n - 1).astype(jnp.int32))


class LineGather:
    def __init__(self, r, c, n, own, full, sends, recvs):
        self.r, self.c, self.n, self.own, self.full = r, c, n, own, full
        self.sends, self.recvs = sends, recvs

    def copy(self, way, k, j):
        block = self.c - k if way == 0 else self.c + k
        to = self.c + 1 if way == 0 else self.c - 1
        src = self.own(j) if k == 0 else self.full(block, j)
        return pltpu.make_async_remote_copy(
            src_ref=src,
            dst_ref=self.full(block, j),
            send_sem=self.sends.at[way, k, j],
            recv_sem=self.recvs.at[way, k, j],
            device_id=(self.r, to),
            device_id_type=MESH,
        )

    def arrives(self, way, k):
        return self.c - 1 - k >= 0 if way == 0 else self.c + 1 + k <= self.n - 1

    def leaves(self, way, k):
        if way == 0:
            return (self.c - k >= 0) & (self.c < self.n - 1)
        return (self.c + k <= self.n - 1) & (self.c > 0)

    def landed(self, way, k, j):
        block = self.c - 1 - k if way == 0 else self.c + 1 + k
        to = self.c + 1 if way == 0 else self.c - 1
        return pltpu.make_async_remote_copy(
            src_ref=self.full(block, j),
            dst_ref=self.full(block, j),
            send_sem=self.sends.at[way, k, j],
            recv_sem=self.recvs.at[way, k, j],
            device_id=(self.r, to),
            device_id_type=MESH,
        )

    def step(self, k, j):
        for way in (0, 1):
            if k > 0:
                pl.when(self.arrives(way, k - 1))(
                    lambda way=way: self.landed(way, k - 1, j).wait_recv()
                )
            if k < self.n - 1:
                pl.when(self.leaves(way, k))(lambda way=way: self.copy(way, k, j).start())

    def drain(self, j):
        for way in (0, 1):
            for k in range(self.n - 1):
                pl.when(self.leaves(way, k))(
                    lambda way=way, k=k: self.copy(way, k, j).wait_send()
                )


class LineScatter:
    def __init__(self, r, c, n, part, land, sends, recvs):
        self.r, self.c, self.n, self.part, self.land = r, c, n, part, land
        self.sends, self.recvs = sends, recvs

    def copy(self, way, b, j):
        to = self.c + 1 if way == 0 else self.c - 1
        return pltpu.make_async_remote_copy(
            src_ref=self.part(b, j),
            dst_ref=self.land(way, b, j),
            send_sem=self.sends.at[way, b, j],
            recv_sem=self.recvs.at[way, b, j],
            device_id=(self.r, to),
            device_id_type=MESH,
        )

    def first(self, way, b, j):
        end = 0 if way == 0 else self.n - 1
        pl.when((self.c == end) & (self.c != b))(lambda: self.copy(way, b, j).start())

    def middle(self, way, b, j):
        here = (self.c > 0) & (self.c < b) if way == 0 else (self.c < self.n - 1) & (self.c > b)

        @pl.when(here)
        def _():
            self.copy(way, b, j).wait_recv()
            part = self.part(b, j)
            part[...] = (part[...].astype(f32) + self.land(way, b, j)[...].astype(f32)).astype(bf16)
            self.copy(way, b, j).start()

    def last(self, j, total):
        total[...] = self.part(self.c, j)[...].astype(f32)
        for way in (0, 1):

            @pl.when(self.c > 0 if way == 0 else self.c < self.n - 1)
            def _(way=way):
                self.copy(way, self.c, j).wait_recv()
                total[...] += self.land(way, self.c, j)[...].astype(f32)

    def drain(self, b, j):
        for way in (0, 1):
            if way == 0:
                sent = (self.c < b) & (self.c < self.n - 1)
            else:
                sent = (self.c > b) & (self.c > 0)
            pl.when(sent)(lambda way=way: self.copy(way, b, j).wait_send())


def scatter_order(n):
    return [(way, n - 1 - k if way == 0 else k) for k in range(n - 1) for way in (0, 1)]


def pieces_of(rows):
    return max(1, rows // 64)


def gather_kernel(n, pieces, x_ref, gain_ref, shift_ref, full_ref, own, sends, recvs, local_sem):
    r, c = lax.axis_index("rows"), lax.axis_index("cols")
    tok = x_ref.shape[0]
    sub = tok // pieces

    def full(b, j):
        return full_ref.at[pl.ds(b * tok + j * sub, sub)]

    gather = LineGather(r, c, n, lambda j: own.at[pl.ds(j * sub, sub)], full, sends, recvs)
    line_barrier(r, c, n)
    for j in range(pieces):
        rows = pl.ds(j * sub, sub)
        normed, _ = normalize(x_ref[rows].astype(f32))
        own[rows] = (normed * gain_ref[...] + shift_ref[...]).astype(bf16)
        gather.step(0, j)
    keep = pltpu.make_async_copy(own, full_ref.at[pl.ds(c * tok, tok)], local_sem)
    keep.start()
    for k in range(1, n):
        for j in range(pieces):
            gather.step(k, j)
    for j in range(pieces):
        gather.drain(j)
    keep.wait()


def gather_normed(n, x, gain, shift):
    tok, width = x.shape
    pieces = pieces_of(tok)
    return pl.pallas_call(
        functools.partial(gather_kernel, n, pieces),
        out_shape=jax.ShapeDtypeStruct((n * tok, width), bf16),
        in_specs=[VM, VM, VM],
        out_specs=HB,
        scratch_shapes=[
            pltpu.VMEM((tok, width), bf16),
            pltpu.SemaphoreType.DMA((2, n - 1, pieces)),
            pltpu.SemaphoreType.DMA((2, n - 1, pieces)),
            pltpu.SemaphoreType.DMA,
        ],
        compiler_params=pltpu.CompilerParams(
            collective_id=1, has_side_effects=True, vmem_limit_bytes=24 * 2**20
        ),
        cost_estimate=pl.CostEstimate(
            flops=10 * tok * width, bytes_accessed=60 * 2**20, transcendentals=0
        ),
        name="gather_normed",
    )(x, gain, shift)


def key_bias(slope, length, keys):
    at = lax.broadcasted_iota(jnp.int32, (1, keys), 1)
    return jnp.where(at < length, slope * LOG2E * at.astype(f32), LOW)


def masked_scores(query, keys, bias, tok, start):
    scores = nt(query, keys) * LOG2E + bias
    row = lax.broadcasted_iota(jnp.int32, (tok, tok), 0)
    col = lax.broadcasted_iota(jnp.int32, (tok, tok), 1)
    tail = jnp.where(col <= row, scores[:, start:], LOW)
    if start == 0:
        return tail
    return jnp.concatenate([scores[:, :start], tail], axis=1)


def attend_block(tok, b, q_ref, k_ref, v_ref, att_ref, lse_ref, slopes_ref, length):
    pairs = q_ref.shape[1] // 128
    extent = (b + 1) * tok
    rows = pl.ds(b * tok, tok)
    lane = lax.broadcasted_iota(jnp.int32, (tok, 128), 1)

    def pair(p, lse_all):
        lanes = pl.ds(pl.multiple_of(p * 128, 128), 128)
        query = q_ref[rows, lanes]
        keys = k_ref[pl.ds(0, extent), lanes]
        values = v_ref[pl.ds(0, extent), lanes]
        results = []
        for u in (0, 1):
            mine = (lane < 64) if u == 0 else (lane >= 64)
            bias = key_bias(slopes_ref[0, 2 * p + u], length, extent)
            scores = masked_scores(
                jnp.where(mine, query, jnp.zeros_like(query)), keys, bias, tok, b * tok
            )
            highest = jnp.max(scores, axis=1, keepdims=True)
            raised = jnp.exp2(scores - highest)
            summed = jnp.sum(raised, axis=1, keepdims=True)
            results.append(nn(raised.astype(bf16), values) * (1.0 / summed))
            total = highest + jnp.log2(summed)
            lse_all = jnp.where(lane == 2 * p + u, total, lse_all)
        att_ref[rows, lanes] = jnp.where(lane < 64, results[0], results[1]).astype(bf16)
        return lse_all

    lse_ref[rows, :] = lax.fori_loop(0, pairs, pair, jnp.zeros((tok, 128), f32))


def attention_kernel(
    n,
    pieces,
    h_ref,
    proj_ref,
    qb_ref,
    vb_ref,
    slopes_ref,
    length_ref,
    outw_ref,
    x_ref,
    outb_ref,
    gain_ref,
    shift_ref,
    cot_ref,
    q_ref,
    k_ref,
    v_ref,
    att_ref,
    lse_ref,
    mid_ref,
    h2_ref,
    dense_ref,
    own,
    part_ref,
    land_ref,
    total,
    g_sends,
    g_recvs,
    s_sends,
    s_recvs,
    local_sem,
):
    r, c = lax.axis_index("rows"), lax.axis_index("cols")
    tok = x_ref.shape[0]
    width = x_ref.shape[1]
    sub = tok // pieces
    length = length_ref[0]

    gather = LineGather(
        r,
        c,
        n,
        lambda j: own.at[pl.ds(j * sub, sub)],
        lambda b, j: dense_ref.at[pl.ds(b * tok + j * sub, sub)],
        g_sends,
        g_recvs,
    )
    scatter = LineScatter(
        r,
        c,
        n,
        lambda b, j: part_ref.at[pl.ds(b * tok + j * sub, sub)],
        lambda way, b, j: land_ref.at[way, pl.ds(b * tok + j * sub, sub)],
        s_sends,
        s_recvs,
    )
    line_barrier(r, c, n)
    for j in range(pieces):
        rows = pl.ds(j * sub, sub)
        live = live_mask(length, c * tok + j * sub, sub)
        own[rows] = (live * cot_ref[rows].astype(f32)).astype(bf16)
        gather.step(0, j)
    keep = pltpu.make_async_copy(own, dense_ref.at[pl.ds(c * tok, tok)], local_sem)
    keep.start()

    def project(b, _):
        rows = pl.ds(pl.multiple_of(b * tok, tok), tok)
        h = h_ref[rows]
        q_ref[rows] = (nn(h, proj_ref[0]) + qb_ref[...]).astype(bf16) * jnp.asarray(0.125, bf16)
        k_ref[rows] = nn(h, proj_ref[1]).astype(bf16)
        v_ref[rows] = (nn(h, proj_ref[2]) + vb_ref[...]).astype(bf16)
        return 0

    lax.fori_loop(0, n, project, 0)

    forward = [(k, j) for k in range(1, n) for j in range(pieces)]
    order = []
    low, high = 0, n - 1
    while low <= high:
        order.append(high)
        if low != high:
            order.append(low)
        low, high = low + 1, high - 1
    for at, b in enumerate(order):
        attend_block(tok, b, q_ref, k_ref, v_ref, att_ref, lse_ref, slopes_ref, length)
        att = att_ref[pl.ds(b * tok, tok)]
        for w in range(width // 512):
            lanes = pl.ds(w * 512, 512)
            part_ref[pl.ds(b * tok, tok), lanes] = nn(att, outw_ref[:, lanes]).astype(bf16)
        for j in range(pieces):
            scatter.first(0, b, j)
            scatter.first(1, b, j)
        if at < len(order) - 1:
            for _ in range(pieces // 2 if n > 2 else 0):
                k, j = forward.pop(0)
                gather.step(k, j)
    for way, b in scatter_order(n):
        for j in range(pieces):
            scatter.middle(way, b, j)
            if way == 1 and forward:
                gather.step(*forward.pop(0))
    while forward:
        gather.step(*forward.pop(0))
    for j in range(pieces):
        rows = pl.ds(j * sub, sub)
        scatter.last(j, total)
        live = live_mask(length, c * tok + j * sub, sub)
        middle = x_ref[rows].astype(f32) + live * (total[...] + outb_ref[...])
        mid_ref[rows] = middle
        normed, _ = normalize(middle)
        h2_ref[rows] = (normed * gain_ref[...] + shift_ref[...]).astype(bf16)
    for j in range(pieces):
        gather.drain(j)
        for b in range(n):
            scatter.drain(b, j)
    keep.wait()


def attention_forward(
    n, h_all, proj, qb, vb, slopes, length, out_w, x, out_b, gain_two, shift_two, cot
):
    tok, width = x.shape
    slab = proj.shape[2]
    rows = n * tok
    pieces = pieces_of(tok)
    shape = jax.ShapeDtypeStruct
    return pl.pallas_call(
        functools.partial(attention_kernel, n, pieces),
        out_shape=(
            shape((rows, slab), bf16),
            shape((rows, slab), bf16),
            shape((rows, slab), bf16),
            shape((rows, slab), bf16),
            shape((rows, 128), f32),
            shape((tok, width), f32),
            shape((tok, width), bf16),
            shape((rows, width), bf16),
        ),
        in_specs=[VM, VM, VM, VM, SM, SM, VM, VM, VM, VM, VM, VM],
        out_specs=(VM, VM, VM, VM, VM, VM, VM, HB),
        scratch_shapes=[
            pltpu.VMEM((tok, width), bf16),
            pltpu.VMEM((rows, width), bf16),
            pltpu.VMEM((2, rows, width), bf16),
            pltpu.VMEM((tok // pieces, width), f32),
            pltpu.SemaphoreType.DMA((2, n - 1, pieces)),
            pltpu.SemaphoreType.DMA((2, n - 1, pieces)),
            pltpu.SemaphoreType.DMA((2, n, pieces)),
            pltpu.SemaphoreType.DMA((2, n, pieces)),
            pltpu.SemaphoreType.DMA,
        ],
        compiler_params=pltpu.CompilerParams(
            collective_id=2, has_side_effects=True, vmem_limit_bytes=58 * 2**20
        ),
        cost_estimate=pl.CostEstimate(
            flops=2 * rows * width * slab * 4 + 4 * rows * rows * slab,
            bytes_accessed=200 * 2**20,
            transcendentals=rows * rows * slab // 64,
        ),
        name="attention_forward",
    )(h_all, proj, qb, vb, slopes, length, out_w, x, out_b, gain_two, shift_two, cot)


def attention_back_block(
    tok, b, q_ref, k_ref, v_ref, att_ref, lse_ref, ga_ref, dq_ref, dk_acc, dv_acc, slopes_ref, length
):
    pairs = q_ref.shape[1] // 128
    extent = (b + 1) * tok
    rows = pl.ds(b * tok, tok)
    lane = lax.broadcasted_iota(jnp.int32, (tok, 128), 1)

    def pair(p, _):
        lanes = pl.ds(pl.multiple_of(p * 128, 128), 128)
        query = q_ref[rows, lanes]
        grads = ga_ref[rows, lanes]
        keys = k_ref[pl.ds(0, extent), lanes]
        values = v_ref[pl.ds(0, extent), lanes]
        product = grads.astype(f32) * att_ref[rows, lanes].astype(f32)
        lse_all = lse_ref[rows, :]
        dq = []
        dk = None
        dv = None
        for u in (0, 1):
            mine = (lane < 64) if u == 0 else (lane >= 64)
            zero = jnp.zeros_like(query)
            own_query = jnp.where(mine, query, zero)
            own_grads = jnp.where(mine, grads, zero)
            bias = key_bias(slopes_ref[0, 2 * p + u], length, extent)
            scores = masked_scores(own_query, keys, bias, tok, b * tok)
            total = jnp.sum(jnp.where(lane == 2 * p + u, lse_all, 0.0), axis=1, keepdims=True)
            inner = jnp.sum(jnp.where(mine, product, 0.0), axis=1, keepdims=True)
            weights = jnp.exp2(scores - total)
            grad_scores = (weights * (nt(own_grads, values) - inner)).astype(bf16)
            dq.append(nn(grad_scores, keys))
            add_dv = tn(weights.astype(bf16), own_grads)
            add_dk = tn(grad_scores, own_query)
            dv = add_dv if dv is None else dv + add_dv
            dk = add_dk if dk is None else dk + add_dk
        dq_ref[rows, lanes] = (jnp.where(lane < 64, dq[0], dq[1]) * 0.125).astype(bf16)
        past = pl.ds(0, extent)
        dk_acc[past, lanes] += dk
        dv_acc[past, lanes] += dv
        return 0

    lax.fori_loop(0, pairs, pair, 0)


def attention_back_kernel(
    n,
    q_ref,
    k_ref,
    v_ref,
    att_ref,
    lse_ref,
    ga_ref,
    slopes_ref,
    length_ref,
    dq_ref,
    dk_ref,
    dv_ref,
    dk_acc,
    dv_acc,
):
    tok = q_ref.shape[0] // n
    length = length_ref[0]
    dk_acc[...] = jnp.zeros_like(dk_acc)
    dv_acc[...] = jnp.zeros_like(dv_acc)
    for b in reversed(range(n)):
        attention_back_block(
            tok, b, q_ref, k_ref, v_ref, att_ref, lse_ref, ga_ref, dq_ref, dk_acc, dv_acc,
            slopes_ref, length,
        )
        rows = pl.ds(b * tok, tok)
        dk_ref[rows] = dk_acc[rows].astype(bf16)
        dv_ref[rows] = dv_acc[rows].astype(bf16)


def attention_backward(n, q, k, v, att, lse, grad_att, slopes, length):
    rows, slab = q.shape
    shape = jax.ShapeDtypeStruct((rows, slab), bf16)
    return pl.pallas_call(
        functools.partial(attention_back_kernel, n),
        out_shape=(shape, shape, shape),
        in_specs=[VM, VM, VM, VM, VM, VM, SM, SM],
        out_specs=(VM, VM, VM),
        scratch_shapes=[pltpu.VMEM((rows, slab), f32), pltpu.VMEM((rows, slab), f32)],
        compiler_params=pltpu.CompilerParams(vmem_limit_bytes=48 * 2**20),
        cost_estimate=pl.CostEstimate(
            flops=10 * rows * rows * slab, bytes_accessed=100 * 2**20,
            transcendentals=rows * rows * slab // 64,
        ),
        name="attention_backward",
    )(q, k, v, att, lse, grad_att, slopes, length)


def gelu_slope(before):
    cumulative = 0.5 * (1.0 + lax.erf(before * (1.0 / math.sqrt(2.0))))
    density = jnp.exp(-0.5 * before * before) * (1.0 / math.sqrt(2.0 * math.pi))
    return cumulative + before * density


def scatter_rows(partial):
    return lax.psum_scatter(partial, "cols", scatter_dimension=0, tiled=True).astype(f32)


def per_device(
    inputs,
    lengths,
    gain_one,
    shift_one,
    projection,
    query_bias,
    value_bias,
    out_weight,
    out_bias,
    gain_two,
    shift_two,
    up_weight,
    up_bias,
    down_weight,
    down_bias,
    cotangent,
):
    n = lax.axis_size("cols")
    c = lax.axis_index("cols")
    tok, width = inputs.shape
    slab = projection.shape[2]
    heads_here = slab // HEAD_DIM
    head_ids = c * heads_here + jnp.arange(heads_here)
    slopes = jnp.exp2(-8.0 * (head_ids + 1).astype(f32) / HEADS).reshape(1, heads_here)
    live = ((c * tok + jnp.arange(tok)) < lengths[0]).astype(f32)[:, None]

    proj = lax.all_gather(jnp.transpose(projection, (1, 0, 2)), "rows", axis=1, tiled=True)
    out_w = lax.all_gather(out_weight, "rows", axis=1, tiled=True)
    up_w = lax.all_gather(up_weight, "rows", axis=0, tiled=True)
    down_w = lax.all_gather(down_weight, "rows", axis=1, tiled=True)

    h_all = gather_normed(n, inputs, gain_one.reshape(1, -1), shift_one.reshape(1, -1))
    q, k, v, att, lse, middle, h_two, dense = attention_forward(
        n,
        h_all,
        proj,
        query_bias.reshape(1, -1),
        value_bias.reshape(1, -1),
        slopes,
        lengths,
        out_w,
        inputs,
        out_bias.reshape(1, -1),
        gain_two.reshape(1, -1),
        shift_two.reshape(1, -1),
        cotangent,
    )
    h2_all = lax.all_gather(h_two, "cols", axis=0, tiled=True)
    before = nn(h2_all, up_w) + up_bias
    active = jax.nn.gelu(before, approximate=False).astype(bf16)
    dense_out = scatter_rows(nn(active, down_w).astype(bf16)) + down_bias
    output = (middle + live * dense_out).astype(bf16)

    grad_active = nt(dense, down_w)
    grad_before = (grad_active * gelu_slope(before)).astype(bf16)
    down_grad = tn(active, dense)
    up_grad = tn(h2_all, grad_before)
    grad_two = scatter_rows(nt(grad_before, up_w).astype(bf16))
    grad_out = cotangent.astype(f32)
    normed_two, inverse_two = normalize(middle)
    gain_two_part = jnp.sum(grad_two * normed_two, axis=0)
    shift_two_part = jnp.sum(grad_two, axis=0)
    grad_middle = grad_out + norm_back(grad_two, normed_two, inverse_two, gain_two)
    grad_branch = (live * grad_middle).astype(bf16)
    branch_all = lax.all_gather(grad_branch, "cols", axis=0, tiled=True)
    out_grad = tn(att, branch_all)
    grad_att = nt(branch_all, out_w).astype(bf16)
    dq, dk, dv = attention_backward(n, q, k, v, att, lse, grad_att, slopes, lengths)
    proj_grad = jnp.stack([tn(h_all, dq), tn(h_all, dk), tn(h_all, dv)], axis=0)
    grad_one = scatter_rows((nt(dq, proj[0]) + nt(dk, proj[1]) + nt(dv, proj[2])).astype(bf16))
    normed_one, inverse_one = normalize(inputs.astype(f32))
    gain_one_part = jnp.sum(grad_one * normed_one, axis=0)
    shift_one_part = jnp.sum(grad_one, axis=0)
    inputs_grad = grad_middle + norm_back(grad_one, normed_one, inverse_one, gain_one)

    def reduced(grad, dim):
        return lax.psum_scatter(grad.astype(bf16), "rows", scatter_dimension=dim, tiled=True).astype(
            f32
        )

    proj_part = jnp.transpose(reduced(proj_grad, 1), (1, 0, 2))
    up_part = reduced(up_grad, 0)
    out_part = reduced(out_grad, 1)
    down_part = reduced(down_grad, 1)

    query_total, value_total, up_bias_total = lax.psum(
        (
            jnp.sum(dq, axis=0, dtype=f32),
            jnp.sum(dv, axis=0, dtype=f32),
            jnp.sum(grad_before, axis=0, dtype=f32),
        ),
        "rows",
    )
    totals = lax.psum(
        (
            gain_one_part,
            shift_one_part,
            gain_two_part,
            shift_two_part,
            jnp.sum(grad_branch, axis=0, dtype=f32),
            jnp.sum(live * grad_out, axis=0, dtype=f32),
        ),
        ("rows", "cols"),
    )
    gain_one_total, shift_one_total, gain_two_total, shift_two_total, out_b_total, down_b_total = (
        totals
    )
    return (
        output,
        inputs_grad,
        gain_one_total,
        shift_one_total,
        proj_part,
        query_total,
        value_total,
        out_part,
        out_b_total,
        gain_two_total,
        shift_two_total,
        up_part,
        up_bias_total,
        down_part,
        down_b_total,
    )


def solution(mesh):
    rows_cols = P(("rows", "cols"), None)
    return jax.shard_map(
        per_device,
        mesh=mesh,
        in_specs=(
            rows_cols,
            P("rows"),
            P(),
            P(),
            P("rows", None, "cols"),
            P("cols"),
            P("cols"),
            P("cols", "rows"),
            P(),
            P(),
            P(),
            P("rows", "cols"),
            P("cols"),
            P("cols", "rows"),
            P(),
            rows_cols,
        ),
        out_specs=(
            rows_cols,
            rows_cols,
            P(),
            P(),
            P("rows", None, "cols"),
            P("cols"),
            P("cols"),
            P("cols", "rows"),
            P(),
            P(),
            P(),
            P("rows", "cols"),
            P("cols"),
            P("cols", "rows"),
            P(),
        ),
        check_vma=False,
    )
```

time: 1190 us -> 980 us (0.82)
  waiting for transfers between devices: 762 us -> 497 us
  Pallas kernels: 0 us -> 218 us
  matrix products: 249 us -> 139 us
  other arithmetic: 82.7 us -> 27.3 us
    all_gather x8 -> x6, waiting for transfers between devices: 418 us -> 163 us  [the longest x1 84.1 us: per_device(): h2_all = lax.all_gather(h_two, 'cols', axis=0, tiled=True)]
    pallas_call x0 -> x3, Pallas kernels: none -> 218 us  [the longest x1 123 us: attention_forward(): pl.pallas_call(functools.partial(attention_kernel, n, pieces), out_shape=...]
    dot_general x18 -> x14, matrix products: 249 us -> 139 us  [the longest x6 49.8 us: nt(): lax.dot_general(a, b, (((1,), (1,)), ((), ())), preferred_element_type=f32)]
    convert_element_type x8 -> x4, other arithmetic: 45 us -> 7.27 us  [the longest x3 7.27 us: reduced(): lax.psum_scatter(grad.astype(bf16), 'rows', scatter_dimension=dim, tiled=...]
    reduce_sum x4 -> x3, other arithmetic: 21.9 us -> 4.85 us  [the longest x1 4.43 us: per_device(): jnp.sum(grad_branch, axis=0, dtype=f32)]
    reduce_scatter x8 -> x7, waiting for transfers between devices: 342 us -> 331 us  [the longest x3 216 us: scatter_rows(): lax.psum_scatter(partial, 'cols', scatter_dimension=0, tiled=True)]
  transfers between devices with their start and end apart: 16 -> 13, of which waited for: 14 -> 10; matrix products, arithmetic and copies ran while one was open for 24% -> 14% of each run, Pallas kernels for 0% -> 22%
where the time goes in v1:
time: 980 us; the launch traced here: 971 us
  waiting for transfers between devices  497 us (51%)
  Pallas kernels  218 us (22%)
  matrix products  139 us (14%)
  blocking collectives  65.4 us (7%)
  other arithmetic  27.3 us (3%)
  between operations  15.3 us (2%)
    reduce_scatter x3, waiting for transfers between devices, scatter_rows(): lax.psum_scatter(partial, 'cols', scatter_dimension=0, tiled=True)  216 us
    pallas_call x1, Pallas kernels, attention_forward(): pl.pallas_call(functools.partial(attention_kernel, n, pieces), out_shape=...  123 us
    reduce_scatter x4, waiting for transfers between devices, reduced(): lax.psum_scatter(grad.astype(bf16), 'rows', scatter_dimension=dim, tiled=...  116 us
    all_gather x1, waiting for transfers between devices, per_device(): h2_all = lax.all_gather(h_two, 'cols', axis=0, tiled=True)  84.1 us
    pallas_call x1, Pallas kernels, gather_normed(): pl.pallas_call(functools.partial(gather_kernel, n, pieces), out_shape=jax...  73.2 us
    all_gather x1, waiting for transfers between devices, per_device(): branch_all = lax.all_gather(grad_branch, 'cols', axis=0, tiled=True)  52.9 us
    dot_general x6, matrix products, nt(): lax.dot_general(a, b, (((1,), (1,)), ((), ())), preferred_element_type=f32)  49.8 us
    dot_general x2, matrix products, nn(): lax.dot_general(a, b, (((1,), (0,)), ((), ())), preferred_element_type=f32)  44.6 us
  transfers between devices with their start and end apart: 13, of which 10 were waited for; matrix products, arithmetic and copies ran while one was open for 14% of the time, Pallas kernels for 22%

profile of v1, /device:TPU:0, one launch (start us, length us, event | category | flops | bytes accessed | tf_op | source)
XLA Modules:
  0.0 971.4 jit_solution(1082607048836672709)
XLA Ops:
  7.2 0.7 all-gather.9.cloned.1.call-update
  8.0 0.7 all-gather.7.cloned.1.call-update
  8.7 0.7 all-gather.13.cloned.1.call-update
  10.1 1.2 copy-done
  11.3 0.7 copy-done.4
  12.0 0.7 copy-done.6
  12.7 73.2 %gather_normed.1.h_ref = bf16[1024,2048]{1,0:T(8,128)(2,1)S(1)} custom-call(bf16[256,2048]{1,0:T(8,128)(2,1)S(1)} %copy-done, f32[1,2048]{1,0:T(1,128)S(1)} %bitcast.52, f32[1,2048]{1,0:T(1,128)S(1)} %bitcast.53), custom_call_target="tpu_custom_call" | custom-call | flops 5242880 | bytes 62914560 | tf_op jit(solution)/shard_map/gather_normed/pallas_call | solution.py:208
  85.9 2.0 copy-done.2
  88.4 122.6 %attention_forward.1 = (bf16[1024,512]{1,0:T(8,128)(2,1)}, bf16[1024,512]{1,0:T(8,128)(2,1)}, bf16[1024,512]{1,0:T(8,128)(2,1)}, bf16[1024,512]{1,0:T(8,128)(2,1...) custom-call(bf16[1024,2048]{1,0:T(8,128)(2,1)} %copy-done.2, ...), custom_call_target="tpu_custom_call" | custom-call | flops 10737418240 | bytes 209715200 | tf_op jit(solution)/shard_map/attention_forward/pallas_call | solution.py:401
  211.7 84.1 %all-gather.11.cloned.1.call-done = bf16[1024,2048]{1,0:T(8,128)(2,1)} async-done(((bf16[256,2048]{1,0:T(8,128)(2,1)}), bf16[1024,2048]{1,0:T(8,128)(2,1)}) %all-gather.11.cloned.1.call-update) | async-done | bytes 4194320 | tf_op jit(solution)/shard_map/all_gather | solution.py:588
  295.8 30.8 %fusion.2 = (bf16[1024,2048]{1,0:T(8,128)(2,1)}, f32[1024,2048]{1,0:T(8,128)}) fusion(f32[2048]{0:T(1024)S(1)} %copy-done.20, bf16[1024,2048]{1,0:T(8,128)(2,1)} %all-gather.11.cloned.1.call-done, bf16[2048,2048]{1,0:T(8,128)(2,1)} %all-gather.13.cloned.1.call-done), kind=kOutput, calls=%fused_computation.4 | convolution fusion | flops 8728346624 | bytes 25174016 | tf_op jit(solution)/shard_map/dot_general | solution.py:25
  326.6 25.4 %all-gather.15.cloned.1.call-done = bf16[2048,2048]{1,0:T(8,128)(2,1)} async-done(((bf16[2048,256]{1,0:T(8,128)(2,1)}), bf16[2048,2048]{1,0:T(8,128)(2,1)}) %all-gather.15.cloned.1.call-update) | async-done | bytes 8388624 | tf_op jit(solution)/shard_map/all_gather | solution.py:570
  352.1 16.4 %convert_reduce_fusion = (f32[2048]{0:T(1024)S(1)}, bf16[1024,2048]{1,0:T(8,128)(2,1)S(1)}) fusion(f32[1024,2048]{1,0:T(8,128)} %get-tuple-element.60, f32[2048]{0:T(1024)S(1)} %copy-done.20, bf16[1024,2048]{1,0:T(8,128)(2,1)} %get-tuple-element.28, bf16[2048,2048]{1,0:T(8,128)(2,1)} %all-gather.15.cloned.1.call-done), kind=kOutput, calls=%fused_computation.11 | convolution fusion | flops 8617195520 | bytes 25182208 | tf_op jit(solution)/shard_map/dot_general | solution.py:29
  368.5 1.9 copy-done.22
  370.4 10.9 %convolution_convert_fusion.2 = bf16[1024,2048]{1,0:T(8,128)(2,1)} fusion(bf16[1024,2048]{1,0:T(8,128)(2,1)S(1)} %get-tuple-element.62, bf16[2048,2048]{1,0:T(8,128)(2,1)S(1)} %copy-done.18), kind=kOutput, calls=%fused_computation.31 | convolution fusion | flops 8592031744 | bytes 16777216 | tf_op jit(solution)/shard_map/dot_general | solution.py:29
  381.3 13.8 %convolution_convert_fusion.3 = bf16[1024,2048]{1,0:T(8,128)(2,1)} fusion(bf16[1024,2048]{1,0:T(8,128)(2,1)} %get-tuple-element.59, bf16[2048,2048]{1,0:T(8,128)(2,1)} %all-gather.15.cloned.1.call-done), kind=kOutput, calls=%fused_computation.32 | convolution fusion | flops 8592031744 | bytes 16777216 | tf_op jit(solution)/shard_map/dot_general | solution.py:25
  395.3 1.5 copy-done.13
  397.3 60.9 %reduce-scatter.10.cloned.1.call-done = bf16[256,2048]{1,0:T(8,128)(2,1)} async-done(((bf16[1024,2048]{1,0:T(8,128)(2,1)}), bf16[256,2048]{1,0:T(8,128)(2,1)}) %reduce-scatter.10.cloned.1.call-update) | async-done | bytes 1048592 | tf_op jit(solution)/shard_map/reduce_scatter | solution.py:537
  458.2 2.2 fusion.37
  460.4 77.5 %reduce-scatter.8.cloned.1.call-done = bf16[256,2048]{1,0:T(8,128)(2,1)} async-done(((bf16[1024,2048]{1,0:T(8,128)(2,1)}), bf16[256,2048]{1,0:T(8,128)(2,1)}) %reduce-scatter.8.cloned.1.call-update) | async-done | bytes 1048592 | tf_op jit(solution)/shard_map/reduce_scatter | solution.py:537
  537.9 4.4 convert_reduce_fusion.4
  542.4 14.2 %convolution_convert_fusion.1 = bf16[2048,2048]{1,0:T(8,128)(2,1)} fusion(bf16[1024,2048]{1,0:T(8,128)(2,1)} %all-gather.11.cloned.1.call-done, bf16[1024,2048]{1,0:T(8,128)(2,1)} %copy-done.22), kind=kOutput, calls=%fused_computation.29 | convolution fusion | flops 8594128896 | bytes 16777216 | tf_op jit(solution)/shard_map/dot_general | solution.py:33
  556.7 14.1 %convolution_convert_fusion = bf16[2048,2048]{1,0:T(8,128)(2,1)} fusion(bf16[1024,2048]{1,0:T(8,128)(2,1)} %get-tuple-element.59, bf16[1024,2048]{1,0:T(8,128)(2,1)} %get-tuple-element.28), kind=kOutput, calls=%fused_computation.28 | convolution fusion | flops 8594128896 | bytes 16777216 | tf_op jit(solution)/shard_map/dot_general | solution.py:33
  570.9 52.9 %all-gather.17.cloned.1.call-done = bf16[1024,2048]{1,0:T(8,128)(2,1)} async-done(((bf16[256,2048]{1,0:T(8,128)(2,1)}), bf16[1024,2048]{1,0:T(8,128)(2,1)}) %all-gather.17.cloned.1.call-update) | async-done | bytes 4194320 | tf_op jit(solution)/shard_map/all_gather | solution.py:605
  623.8 6.1 convolution_convert_fusion.4
  630.2 6.3 convolution_convert_fusion.8.ga_ref
  636.5 22.3 %attention_backward.1 = (bf16[1024,512]{1,0:T(8,128)(2,1)S(1)}, bf16[1024,512]{1,0:T(8,128)(2,1)S(1)}, bf16[1024,512]{1,0:T(8,128)(2,1)S(1)}) custom-call(bf16[1024,512]{1,0:T(8,128)(2,1)S(1)} %copy-done.10, bf16[1024,512]{1,0:T(8,128)(2,1)S(1)} %copy-done.11, bf16[1024,512]{1,0:T(8,128)(2,1)} %get-tuple-element.31.v_ref, ...), custom_call_target="tpu_custom_call" | custom-call | flops 5368709120 | bytes 104857600 | tf_op jit(solution)/shard_map/attention_backward/pallas_call | solution.py:515
  658.9 2.4 fusion.39
  661.2 5.6 fusion.40
  666.8 8.3 add_convert_fusion
  675.4 4.8 fusion.22
  680.3 2.5 fusion.23
  682.7 2.5 fusion.24
  685.2 3.1 pad_maximum_fusion
  688.4 1.2 copy-done.1
  690.3 6.8 reduce-scatter.18.cloned.1.call-done
  697.1 2.8 convert_element_type.109
  699.9 72.2 %reduce-scatter.20.cloned.1.call-done = bf16[2048,256]{1,0:T(8,128)(2,1)} async-done(((bf16[2048,2048]{1,0:T(8,128)(2,1)}), bf16[2048,256]{1,0:T(8,128)(2,1)}) %reduce-scatter.20.cloned.1.call-update) | async-done | bytes 1048592 | tf_op jit(solution)/shard_map/reduce_scatter | solution.py:617
  772.1 2.7 convert_element_type.112
  775.2 23.2 %all-reduce.1 = (f32[512]{0:T(512)}, f32[512]{0:T(512)}, f32[2048]{0:T(1024)}) all-reduce(f32[512]{0:T(512)S(1)} %convert_reduce_fusion.6, f32[512]{0:T(512)S(1)} %convert_reduce_fusion.5, f32[2048]{0:T(1024)S(1)} %get-tuple-element.61), channel_id=1, replica_groups=mesh['rows'=8,'cols'=4] {'rows'}, use_global_device_ids=true, to_apply=%region_17.0 | all-reduce | flops 3072 | bytes 24576 | tf_op jit(solution)/shard_map/psum | solution.py:626
  798.4 18.2 %reduce-scatter.16.cloned.1.call-done = bf16[512,256]{1,0:T(8,128)(2,1)} async-done(((bf16[512,2048]{1,0:T(8,128)(2,1)}), bf16[512,256]{1,0:T(8,128)(2,1)}) %reduce-scatter.16.cloned.1.call-update) | async-done | bytes 262160 | tf_op jit(solution)/shard_map/reduce_scatter | solution.py:617
  816.6 1.8 convert_element_type.106
  818.4 77.3 %reduce-scatter.12.cloned.1.call-done = bf16[256,2048]{1,0:T(8,128)(2,1)} async-done(((bf16[1024,2048]{1,0:T(8,128)(2,1)}), bf16[256,2048]{1,0:T(8,128)(2,1)}) %reduce-scatter.12.cloned.1.call-update) | async-done | bytes 1048592 | tf_op jit(solution)/shard_map/reduce_scatter | solution.py:537
  895.7 2.3 fusion.38
  898.0 42.3 %all-reduce = (f32[2048]{0:T(1024)}, f32[2048]{0:T(1024)}, f32[2048]{0:T(1024)}, f32[2048]{0:T(1024)}, f32[2048]{0:T(1024)}, /*index=5*/f32[2048]{0:T(1024)}) all-reduce(f32[2048]{0:T(1024)S(1)} %get-tuple-element.39, f32[2048]{0:T(1024)S(1)} %get-tuple-element.44, ...), channel_id=1, replica_groups=mesh['rows'=8,'cols'=4] {'rows','cols'}, use_global_device_ids=true, to_apply=%region_12.0 | all-reduce | flops 12288 | bytes 98304 | tf_op jit(solution)/shard_map/psum | solution.py:634
  940.2 3.4 fusion.30
  943.6 18.4 %reduce-scatter.14.cloned.1.call-done = bf16[3,256,512]{2,1,0:T(8,128)(2,1)} async-done(((bf16[3,2048,512]{2,1,0:T(8,128)(2,1)}), bf16[3,256,512]{2,1,0:T(8,128)(2,1)}) %reduce-scatter.14.cloned.1.call-update) | async-done | bytes 786448 | tf_op jit(solution)/shard_map/reduce_scatter | solution.py:617
  962.0 2.5 convert_bitcast_fusion
  (85 shorter events, 3.9 us)
Async XLA Ops:
  7.2 81.2 %all-gather.9.cloned.1.call-start = ((), (), s32[]{:S(2)}) async-start(), calls=%async_computation.8 | async-start | bytes 2359296 | tf_op jit(solution)/shard_map/all_gather | solution.py:568
  7.9 80.5 %all-gather.7.cloned.1.call-start = ((), (), s32[]{:S(2)}) async-start(), calls=%async_computation.7 | async-start | bytes 7077888 | tf_op jit(solution)/shard_map/all_gather | solution.py:567
  8.7 203.0 %all-gather.13.cloned.1.call-start = ((), (), s32[]{:S(2)}) async-start(), calls=%async_computation.10 | async-start | bytes 9437184 | tf_op jit(solution)/shard_map/all_gather | solution.py:569
  9.4 286.4 %all-gather.11.cloned.1.call-start = ((), (), s32[]{:S(2)}) async-start(), calls=%async_computation.9 | async-start | bytes 5242880 | tf_op jit(solution)/shard_map/all_gather | solution.py:588
  10.1 1.2 copy-start
  11.3 0.7 copy-start.4
  12.0 0.7 copy-start.6
  85.9 2.0 copy-start.2
  88.4 207.4 %copy-start.20 = (f32[2048]{0:T(1024)S(1)}, f32[2048]{0:T(1024)}, u32[]{:S(2)}) copy-start(f32[2048]{0:T(1024)} %param.28) | copy-start | bytes 24580
  211.0 141.0 %all-gather.15.cloned.1.call-start = ((), (), s32[]{:S(2)}) async-start(), calls=%async_computation.11 | async-start | bytes 9437184 | tf_op jit(solution)/shard_map/all_gather | solution.py:570
  211.6 246.6 %reduce-scatter.10.cloned.1.call-start = ((), (), s32[]{:S(2)}) async-start(), calls=%async_computation.13 | async-start | bytes 5242880 | tf_op jit(solution)/shard_map/reduce_scatter | solution.py:537
  352.1 18.3 %copy-start.18 = (bf16[2048,2048]{1,0:T(8,128)(2,1)S(1)}, bf16[2048,2048]{1,0:T(8,128)(2,1)}, u32[]{:S(2)}) copy-start(bf16[2048,2048]{1,0:T(8,128)(2,1)} %all-gather.13.cloned.1.call-done) | copy-start | bytes 25165828
  368.5 1.9 copy-start.22
  381.3 156.6 %reduce-scatter.8.cloned.1.call-start = ((), (), s32[]{:S(2)}) async-start(), calls=%async_computation.12 | async-start | bytes 5242880 | tf_op jit(solution)/shard_map/reduce_scatter | solution.py:537
  395.2 1.6 copy-start.13
  395.2 63.0 %copy-start.16 = (f32[2048]{0:T(1024)S(1)}, f32[2048]{0:T(1024)}, u32[]{:S(2)}) copy-start(f32[2048]{0:T(1024)} %param.25) | copy-start | bytes 24580
  395.2 142.7 %copy-start.15 = (bf16[256,2048]{1,0:T(8,128)(2,1)S(1)}, bf16[256,2048]{1,0:T(8,128)(2,1)}, u32[]{:S(2)}) copy-start(bf16[256,2048]{1,0:T(8,128)(2,1)} %cot_ref.1) | copy-start | bytes 3145732
  395.2 142.7 %copy-start.17 = (f32[2048]{0:T(1024)S(1)}, f32[2048]{0:T(1024)}, u32[]{:S(2)}) copy-start(f32[2048]{0:T(1024)} %param.30) | copy-start | bytes 24580
  395.2 228.6 %all-gather.17.cloned.1.call-start = ((), (), s32[]{:S(2)}) async-start(), calls=%async_computation.14 | async-start | bytes 5242880 | tf_op jit(solution)/shard_map/all_gather | solution.py:605
  542.4 154.7 %reduce-scatter.18.cloned.1.call-start = ((), (), s32[]{:S(2)}) async-start(), calls=%async_computation.18 | async-start | bytes 9437184 | tf_op jit(solution)/shard_map/reduce_scatter | solution.py:617
  556.7 215.4 %reduce-scatter.20.cloned.1.call-start = ((), (), s32[]{:S(2)}) async-start(), calls=%async_computation.19 | async-start | bytes 9437184 | tf_op jit(solution)/shard_map/reduce_scatter | solution.py:617
  570.8 53.0 %copy-start.21 = (bf16[1024,512]{1,0:T(8,128)(2,1)S(1)}, bf16[1024,512]{1,0:T(8,128)(2,1)}, u32[]{:S(2)}) copy-start(bf16[1024,512]{1,0:T(8,128)(2,1)} %get-tuple-element.32.att_ref) | copy-start | bytes 3145732
  570.8 245.8 %reduce-scatter.16.cloned.1.call-start = ((), (), s32[]{:S(2)}) async-start(), calls=%async_computation.17 | async-start | bytes 2359296 | tf_op jit(solution)/shard_map/reduce_scatter | solution.py:617
  623.8 6.4 copy-start.19
  629.9 6.6 copy-start.7
  629.9 6.6 copy-start.12
  629.9 265.8 %reduce-scatter.12.cloned.1.call-start = ((), (), s32[]{:S(2)}) async-start(), calls=%async_computation.15 | async-start | bytes 5242880 | tf_op jit(solution)/shard_map/reduce_scatter | solution.py:537
  630.2 6.3 copy-start.10
  630.2 6.3 copy-start.11
  630.2 28.6 %slice-start = ((s8[6291456]{0:T(1024)(128)(4,1)}), s8[4194304]{0:T(1024)(128)(4,1)S(1)}, s32[]{:S(2)}) async-start(s8[6291456]{0:T(1024)(128)(4,1)} %bitcast.55), calls=%async_computation.20 | async-start | bytes 8388608
  636.5 22.3 %slice-start.1 = ((s8[6291456]{0:T(1024)(128)(4,1)}), s8[2097152]{0:T(1024)(128)(4,1)S(1)}, s32[]{:S(2)}) async-start(s8[6291456]{0:T(1024)(128)(4,1)} %bitcast.55), calls=%async_computation.21 | async-start | bytes 4194304
  658.8 2.4 copy-start.8
  675.1 5.1 copy-start.9
  675.1 286.9 %reduce-scatter.14.cloned.1.call-start = ((), (), s32[]{:S(2)}) async-start(), calls=%async_computation.16 | async-start | bytes 7077888 | tf_op jit(solution)/shard_map/reduce_scatter | solution.py:617
  675.4 4.8 copy-start.3
  688.3 1.3 copy-start.1
  690.3 205.4 %copy-start.5 = (f32[2048]{0:T(1024)S(1)}, f32[2048]{0:T(1024)}, u32[]{:S(2)}) copy-start(f32[2048]{0:T(1024)} %param.18) | copy-start | bytes 24580
  775.2 165.0 %copy-start.14 = (f32[256,2048]{1,0:T(8,128)S(1)}, f32[256,2048]{1,0:T(8,128)}, u32[]{:S(2)}) copy-start(f32[256,2048]{1,0:T(8,128)} %get-tuple-element.56) | copy-start | bytes 6291460
Sparse Core Ops, SparseCore 0:
  9.9 30.8 all-gather.8
  42.7 45.5 all-gather.6
  90.2 54.3 all-gather.12
  211.1 84.6 all-gather.10
  297.5 54.4 all-gather.14
  381.4 76.7 reduce-scatter.9
  460.6 77.2 reduce-scatter.7
  542.5 81.2 all-gather.16
  627.2 69.7 reduce-scatter.17
  700.8 71.2 reduce-scatter.19
  775.4 41.2 reduce-scatter.15
  818.9 76.7 reduce-scatter.11
  899.1 62.8 reduce-scatter.13
